TPU v7x, 32 devices: a whole 2x2x4 slice. The times are simulated.
32 devices in a mesh: wide: 8 (over y, x, core), narrow: 4 (over z).
Axes of the slice: x: 2, y: 2, z: 4, core: 2. Of those that a mesh axis runs over, the one named last changes fastest.
Arguments:
- features: bfloat16 [131072, 602], P(('wide', 'narrow')), may hold values from -6 to 6
- tile_src: int32 [1024, 12], P(('wide', 'narrow')), may hold values from 0 to 33, as said below
- edge_weight: bfloat16 [1024, 12, 128, 128], P(('wide', 'narrow')), may hold values from -0.044189453 to 0.044189453
- send_lists: int32 [32, 32, 8], P(('wide', 'narrow')), may hold values from -1 to 4095, as said below
- labels: int32 [131072], P(('wide', 'narrow')), may hold values from 0 to 40
- train_mask: int32 [131072], P(('wide', 'narrow')), may hold values from 0 to 1, as said below
- w_in: float32 [602, 512], replicated, may hold values from -0.25 to 0.25
- w_pair: float32 [1, 2, 512, 512], replicated, may hold values from -0.25 to 0.25
- w_cat: float32 [1, 1024, 512], replicated, may hold values from -0.1875 to 0.1875
- w_out: float32 [512, 41], replicated, may hold values from -0.25 to 0.25
- m_in: float32 [602, 512], replicated, may hold values from -2.861023e-06 to 2.861023e-06
- m_pair: float32 [1, 2, 512, 512], replicated, may hold values from -2.861023e-06 to 2.861023e-06
- m_cat: float32 [1, 1024, 512], replicated, may hold values from -2.861023e-06 to 2.861023e-06
- m_out: float32 [512, 41], replicated, may hold values from -2.861023e-06 to 2.861023e-06
- v_in: float32 [602, 512], replicated, may hold values from 2.903196e-15 to 1.1612784e-14
- v_pair: float32 [1, 2, 512, 512], replicated, may hold values from 2.903196e-15 to 1.1612784e-14
- v_cat: float32 [1, 1024, 512], replicated, may hold values from 2.903196e-15 to 1.1612784e-14
- v_out: float32 [512, 41], replicated, may hold values from 2.903196e-15 to 1.1612784e-14
Outputs:
- new_w_in: float32 [602, 512], replicated
- new_w_pair: float32 [1, 2, 512, 512], replicated
- new_w_cat: float32 [1, 1024, 512], replicated
- new_w_out: float32 [512, 41], replicated
- new_m_in: float32 [602, 512], replicated
- new_m_pair: float32 [1, 2, 512, 512], replicated
- new_m_cat: float32 [1, 1024, 512], replicated
- new_m_out: float32 [512, 41], replicated
- new_v_in: float32 [602, 512], replicated
- new_v_pair: float32 [1, 2, 512, 512], replicated
- new_v_cat: float32 [1, 1024, 512], replicated
- new_v_out: float32 [512, 41], replicated
- loss_sum: float32 [], replicated
- train_count: float32 [], replicated
- grad_norm: float32 [], replicated
Inputs may be any that keep to these rules, and one draw needn't show every extreme that they name: `send_lists`: entry [q, p, s] is one of device q's 4096 owned rows (numbered from 0) that device q sends to device p in slot s, or -1 for an empty slot; empty slots stand after used ones; each list has 1 to 8 used slots, and every device has a full list. `tile_src`: entries index the 34 blocks of the owning device's rows followed by its received rows in order of sending device and slot; every block is named on every device. `train_mask`: node 0 is a training node.
All inputs are finite; a program needn't handle non-finite values.
Results may differ from a plain program's by a relative error of at most 0.018.
Values may be sent and summed in bfloat16 or wider, within the bound.
No kernel may reach another device: no remote copies, remote signals or barrier semaphores. Data moves between devices by JAX's collectives and lax.ppermute only.
A program may use at most 192 MiB of HBM per device.

v0:
```python
import jax
import jax.numpy as jnp
from jax import lax
from jax.sharding import PartitionSpec as P

ADAM_STEP = 10


NORM_EPS = 1e-06
SMOOTHING = 0.1
CLIP_AT = 0.002
LEARN_RATE = 0.05
BETA_FIRST = 0.9
BETA_SECOND = 0.999
ADAM_EPS = 1e-08
WEIGHT_DECAY = 0.01
HIGHEST = lax.Precision.HIGHEST


def adam_update(weight, grad, first, second):
    first_new = BETA_FIRST * first + (1.0 - BETA_FIRST) * grad
    second_new = BETA_SECOND * second + (1.0 - BETA_SECOND) * grad * grad
    first_hat = first_new / (1.0 - BETA_FIRST**ADAM_STEP)
    second_hat = second_new / (1.0 - BETA_SECOND**ADAM_STEP)
    weight_new = weight - LEARN_RATE * (
        first_hat / (jnp.sqrt(second_hat) + ADAM_EPS) + WEIGHT_DECAY * weight
    )
    return (first_new, second_new, weight_new)


def inner_rows(left, right):
    return lax.dot_general(
        left, right, (((0,), (0,)), ((), ())), preferred_element_type=jnp.float32
    )


def rescale(mixed):
    active = jax.nn.gelu(mixed, approximate=True)
    return active * lax.rsqrt(jnp.mean(active * active, axis=1, keepdims=True) + NORM_EPS)


def slot_picker(slot_lists, node_rows):
    row_ids = jnp.arange(node_rows, dtype=jnp.int32)
    return slot_lists.reshape(-1)[:, None] == row_ids[None, :]


def block_picker(sources, column, total_blocks):
    source_now = lax.dynamic_index_in_dim(sources, column, 1, keepdims=False)
    block_ids = jnp.arange(total_blocks, dtype=jnp.int32)
    return source_now[:, None] == block_ids[None, :]


def halo_send(outgoing):
    return lax.all_to_all(outgoing, ("wide", "narrow"), split_axis=0, concat_axis=0, tiled=True)


def halo_return(returning):
    return lax.all_to_all(
        returning.astype(jnp.bfloat16), ("wide", "narrow"), split_axis=0, concat_axis=0, tiled=True
    ).astype(returning.dtype)


def layer_forward(inputs_b, slot_lists, sources, edge_weight, pair_b, cat_b):
    node_rows, hidden_width = inputs_b.shape
    tile_rows = edge_weight.shape[2]
    picker = slot_picker(slot_lists, node_rows).astype(jnp.bfloat16)
    outgoing = jnp.dot(picker, inputs_b, preferred_element_type=jnp.float32).astype(jnp.bfloat16)
    incoming = halo_send(outgoing.reshape(slot_lists.shape + (hidden_width,)))
    extended = jnp.concatenate([inputs_b, incoming.reshape(-1, hidden_width)], axis=0)
    extended = extended.reshape(-1, tile_rows, hidden_width)
    total_blocks = extended.shape[0]

    def add_tile(column, accum):
        choose = block_picker(sources, column, total_blocks).astype(jnp.bfloat16)
        selected = jnp.einsum(
            "bx,xjh->bjh", choose, extended, preferred_element_type=jnp.float32
        ).astype(jnp.bfloat16)
        weights_now = lax.dynamic_index_in_dim(edge_weight, column, 1, keepdims=False)
        return accum + jnp.einsum(
            "bij,bjh->bih", weights_now, selected, preferred_element_type=jnp.float32
        )

    summed = jnp.zeros((sources.shape[0], tile_rows, hidden_width), jnp.float32)
    summed = lax.fori_loop(0, sources.shape[1], add_tile, summed)
    agg_b = summed.reshape(node_rows, hidden_width).astype(jnp.bfloat16)
    own_part = jnp.dot(inputs_b, pair_b[0], preferred_element_type=jnp.float32)
    neighbour = jnp.dot(agg_b, pair_b[1], preferred_element_type=jnp.float32)
    joined_b = jnp.concatenate([own_part, neighbour], axis=1).astype(jnp.bfloat16)
    mixed = jnp.dot(joined_b, cat_b, preferred_element_type=jnp.float32)
    return (rescale(mixed), (agg_b, joined_b, mixed))


def layer_backward(grad_output, inputs_b, kept, slot_lists, sources, edge_weight, pair_b, cat_b):
    agg_b, joined_b, mixed = kept
    node_rows, hidden_width = inputs_b.shape
    tile_rows = edge_weight.shape[2]
    halo_count = slot_lists.shape[0] * slot_lists.shape[1]
    _, pull = jax.vjp(rescale, mixed)
    grad_mixed = pull(grad_output)[0].astype(jnp.bfloat16)
    grad_cat = inner_rows(joined_b, grad_mixed)
    grad_joined = jnp.dot(grad_mixed, cat_b.T, preferred_element_type=jnp.float32).astype(
        jnp.bfloat16
    )
    grad_own = grad_joined[:, :hidden_width]
    grad_neigh = grad_joined[:, hidden_width:]
    grad_pair = jnp.stack([inner_rows(inputs_b, grad_own), inner_rows(agg_b, grad_neigh)])
    grad_agg = jnp.dot(grad_neigh, pair_b[1].T, preferred_element_type=jnp.float32).astype(
        jnp.bfloat16
    )
    grad_agg = grad_agg.reshape(-1, tile_rows, hidden_width)
    total_blocks = (node_rows + halo_count) // tile_rows

    def add_tile(column, accum):
        weights_now = lax.dynamic_index_in_dim(edge_weight, column, 1, keepdims=False)
        term = jnp.einsum("bij,bih->bjh", weights_now, grad_agg, preferred_element_type=jnp.float32)
        choose = block_picker(sources, column, total_blocks).astype(jnp.float32)
        return accum + jnp.einsum(
            "bx,bjh->xjh", choose, term, precision=HIGHEST, preferred_element_type=jnp.float32
        )

    grad_ext = jnp.zeros((total_blocks, tile_rows, hidden_width), jnp.float32)
    grad_ext = lax.fori_loop(0, sources.shape[1], add_tile, grad_ext).reshape(-1, hidden_width)
    grad_input = grad_ext[:node_rows] + jnp.dot(
        grad_own, pair_b[0].T, preferred_element_type=jnp.float32
    )
    returned = halo_return(grad_ext[node_rows:].reshape(slot_lists.shape + (hidden_width,)))
    picker = slot_picker(slot_lists, node_rows).astype(jnp.float32)
    grad_input = grad_input + lax.dot_general(
        picker,
        returned.reshape(-1, hidden_width),
        (((0,), (0,)), ((), ())),
        precision=HIGHEST,
        preferred_element_type=jnp.float32,
    )
    return (grad_input, grad_pair, grad_cat)


def flatten_all(arrays):
    return jnp.concatenate([member.reshape(-1) for member in arrays])


def unflatten_all(flat, like):
    pieces = []
    offset = 0
    for member in like:
        pieces.append(flat[offset : offset + member.size].reshape(member.shape))
        offset = offset + member.size
    return pieces


def shards(
    features,
    tile_src,
    edge_weight,
    send_lists,
    labels,
    train_mask,
    w_in,
    w_pair,
    w_cat,
    w_out,
    m_in,
    m_pair,
    m_cat,
    m_out,
    v_in,
    v_pair,
    v_cat,
    v_out,
):
    slot_lists = send_lists[0]
    in_b = w_in.astype(jnp.bfloat16)
    pair_all = w_pair.astype(jnp.bfloat16)
    cat_all = w_cat.astype(jnp.bfloat16)
    out_b = w_out.astype(jnp.bfloat16)
    class_count = out_b.shape[1]
    hidden_b = jnp.dot(features, in_b, preferred_element_type=jnp.float32).astype(jnp.bfloat16)
    layer_index = 0
    inputs_seen = [hidden_b]
    normed, kept = layer_forward(
        hidden_b, slot_lists, tile_src, edge_weight, pair_all[layer_index], cat_all[layer_index]
    )
    kept_all = [kept]
    hidden_b = normed.astype(jnp.bfloat16)
    logits = jnp.dot(hidden_b, out_b, preferred_element_type=jnp.float32)
    log_prob = jax.nn.log_softmax(logits, axis=-1)
    smoothed = (1.0 - SMOOTHING) * jax.nn.one_hot(
        labels, class_count, dtype=jnp.float32
    ) + SMOOTHING / class_count
    mask_vals = train_mask.astype(jnp.float32)
    local_loss = jnp.sum(-jnp.sum(smoothed * log_prob, axis=-1) * mask_vals)
    loss_sum, train_count = lax.psum((local_loss, jnp.sum(mask_vals)), ("wide", "narrow"))
    grad_logits = ((jnp.exp(log_prob) - smoothed) * (mask_vals / train_count)[:, None]).astype(
        jnp.bfloat16
    )
    grad_out = inner_rows(hidden_b, grad_logits)
    grad_hidden = jnp.dot(grad_logits, out_b.T, preferred_element_type=jnp.float32)
    pair_grads = []
    cat_grads = []
    for layer_index in reversed(range(len(kept_all))):
        grad_hidden, grad_pair_now, grad_cat_now = layer_backward(
            grad_hidden,
            inputs_seen[layer_index],
            kept_all[layer_index],
            slot_lists,
            tile_src,
            edge_weight,
            pair_all[layer_index],
            cat_all[layer_index],
        )
        pair_grads.insert(0, grad_pair_now)
        cat_grads.insert(0, grad_cat_now)
    grad_in = inner_rows(features, grad_hidden.astype(jnp.bfloat16))
    params = [w_in, w_pair, w_cat, w_out]
    flat_grad = flatten_all([grad_in, jnp.stack(pair_grads), jnp.stack(cat_grads), grad_out])
    flat_weight = flatten_all(params)
    flat_first = flatten_all([m_in, m_pair, m_cat, m_out])
    flat_second = flatten_all([v_in, v_pair, v_cat, v_out])
    summed = lax.psum(flat_grad, ("wide", "narrow"))
    grad_norm = jnp.sqrt(jnp.sum(summed * summed))
    scale = CLIP_AT / jnp.maximum(grad_norm, CLIP_AT)
    new_first, new_second, new_weight = adam_update(
        flat_weight, summed * scale, flat_first, flat_second
    )
    weights_out = unflatten_all(new_weight, params)
    firsts_out = unflatten_all(new_first, params)
    seconds_out = unflatten_all(new_second, params)
    return (
        weights_out[0],
        weights_out[1],
        weights_out[2],
        weights_out[3],
        firsts_out[0],
        firsts_out[1],
        firsts_out[2],
        firsts_out[3],
        seconds_out[0],
        seconds_out[1],
        seconds_out[2],
        seconds_out[3],
        loss_sum,
        train_count,
        grad_norm,
    )


def solution(mesh):
    in_specs = (
        P(("wide", "narrow"), None),
        P(("wide", "narrow"), None),
        P(("wide", "narrow"), None, None, None),
        P(("wide", "narrow"), None, None),
        P(("wide", "narrow")),
        P(("wide", "narrow")),
        P(),
        P(),
        P(),
        P(),
        P(),
        P(),
        P(),
        P(),
        P(),
        P(),
        P(),
        P(),
    )
    out_specs = (P(), P(), P(), P(), P(), P(), P(), P(), P(), P(), P(), P(), P(), P(), P())
    return jax.shard_map(shards, mesh=mesh, in_specs=in_specs, out_specs=out_specs, check_vma=False)
```

profile of v0, /device:TPU:0, one launch (start us, length us, event | category | flops | bytes accessed | tf_op | source)
XLA Modules:
  0.0 903.6 jit_solution(11568033809584587080)
XLA Ops:
  8.0 6.3 convolution_convert_fusion.4
  18.3 7.4 all-to-all-start
  41.7 215.5 %while.28 = (s32[]{:T(128)}, f32[32,128,512]{2,1,0:T(8,128)}, bf16[32,12,128,128]{3,2,1,0:T(8,128)(2,1)}, s32[32,12]{0,1:T(8,128)}, bf16[34,128,512]{2,1,0:T(8,128)(2,1)}, /*index=5*/s32[]{:T(128)}, s32[]{:T(128)}) while((s32[]{:T(128)}, f32[32,128,512]{2,1,0:T(8,128)}, bf16[32,12,128,128]{3,2,1,0:T(8,128)(2,1)}, ...), condition=%wide.region_1.2_spmd.clone, body=%wide.region_0.1_spmd.clone.sunk | while | flops 683672640 | bytes 97780248 | solution.py:84
  42.7 6.2 fusion.95
  49.0 7.6 select_add_fusion.5
  60.7 6.2 fusion.95
  66.9 7.6 select_add_fusion.5
  78.6 6.2 fusion.95
  84.8 7.6 select_add_fusion.5
  96.5 6.2 fusion.95
  102.7 7.6 select_add_fusion.5
  114.4 6.2 fusion.95
  120.6 7.6 select_add_fusion.5
  132.3 6.2 fusion.95
  138.5 7.6 select_add_fusion.5
  150.2 6.2 fusion.95
  156.4 7.6 select_add_fusion.5
  168.1 6.2 fusion.95
  174.3 7.6 select_add_fusion.5
  186.0 6.2 fusion.95
  192.2 7.6 select_add_fusion.5
  210.2 7.6 select_add_fusion.5
  228.1 7.6 select_add_fusion.5
  246.0 7.6 select_add_fusion.5
  266.1 7.2 multiply_reduce_fusion.1
  277.8 40.7 %all-reduce = (f32[]{:T(128)}, f32[]{:T(128)}) all-reduce(f32[]{:T(128)} %get-tuple-element.267, f32[]{:T(128)} %get-tuple-element.266), channel_id=1, replica_groups=mesh['wide'=8,'narrow'=4] {'wide','narrow'}, use_global_device_ids=true, to_apply=%region_6.7 | all-reduce | flops 2 | bytes 16 | tf_op jit(solution)/shard_map/psum | solution.py:192
  319.2 6.8 fusion.44
  331.9 7.0 fusion.26
  363.1 269.4 %while.29 = (s32[]{:T(128)}, f32[34,128,512]{2,0,1:T(8,128)}, s32[32,12]{0,1:T(8,128)}, bf16[32,12,128,128]{3,2,1,0:T(8,128)(2,1)}, bf16[32,128,512]{2,1,0:T(8,128)(2,1)}, /*index=5*/s32[]{:T(128)}, s32[]{:T(128)}) while((s32[]{:T(128)}, f32[34,128,512]{2,0,1:T(8,128)}, s32[32,12]{0,1:T(8,128)}, ...), condition=%wide.region_9.10_spmd.clone, body=%wide.region_8.9_spmd.clone.sunk | while | flops 1396966400 | bytes 111149592 | solution.py:122
  369.0 12.8 %select_add_fusion.6 = f32[34,128,512]{2,0,1:T(8,128)S(1)} fusion(f32[34,128,512]{2,0,1:T(8,128)S(1)} %copy-done, pred[]{:T(512)S(6)} %compare.7, f32[32,128,512]{2,1,0:T(8,128)S(1)} %fusion.100, s32[32]{0:T(128)S(1)} %dynamic-slice_bitcast_fusion.5), kind=kOutput, calls=%fused_computation.12.clone.1 | convolution fusion | flops 860095552 | bytes 26214528 | tf_op jit(solution)/shard_map/while/body/eval_jaxpr/bx,bjh->xjh/dot_general | solution.py:117
  391.5 12.8 %select_add_fusion.6 = f32[34,128,512]{2,0,1:T(8,128)S(1)} fusion(f32[34,128,512]{2,0,1:T(8,128)S(1)} %copy-done, pred[]{:T(512)S(6)} %compare.7, f32[32,128,512]{2,1,0:T(8,128)S(1)} %fusion.100, s32[32]{0:T(128)S(1)} %dynamic-slice_bitcast_fusion.5), kind=kOutput, calls=%fused_computation.12.clone.1 | convolution fusion | flops 860095552 | bytes 26214528 | tf_op jit(solution)/shard_map/while/body/eval_jaxpr/bx,bjh->xjh/dot_general | solution.py:117
  413.9 12.8 %select_add_fusion.6 = f32[34,128,512]{2,0,1:T(8,128)S(1)} fusion(f32[34,128,512]{2,0,1:T(8,128)S(1)} %copy-done, pred[]{:T(512)S(6)} %compare.7, f32[32,128,512]{2,1,0:T(8,128)S(1)} %fusion.100, s32[32]{0:T(128)S(1)} %dynamic-slice_bitcast_fusion.5), kind=kOutput, calls=%fused_computation.12.clone.1 | convolution fusion | flops 860095552 | bytes 26214528 | tf_op jit(solution)/shard_map/while/body/eval_jaxpr/bx,bjh->xjh/dot_general | solution.py:117
  436.3 12.8 %select_add_fusion.6 = f32[34,128,512]{2,0,1:T(8,128)S(1)} fusion(f32[34,128,512]{2,0,1:T(8,128)S(1)} %copy-done, pred[]{:T(512)S(6)} %compare.7, f32[32,128,512]{2,1,0:T(8,128)S(1)} %fusion.100, s32[32]{0:T(128)S(1)} %dynamic-slice_bitcast_fusion.5), kind=kOutput, calls=%fused_computation.12.clone.1 | convolution fusion | flops 860095552 | bytes 26214528 | tf_op jit(solution)/shard_map/while/body/eval_jaxpr/bx,bjh->xjh/dot_general | solution.py:117
  458.7 12.8 %select_add_fusion.6 = f32[34,128,512]{2,0,1:T(8,128)S(1)} fusion(f32[34,128,512]{2,0,1:T(8,128)S(1)} %copy-done, pred[]{:T(512)S(6)} %compare.7, f32[32,128,512]{2,1,0:T(8,128)S(1)} %fusion.100, s32[32]{0:T(128)S(1)} %dynamic-slice_bitcast_fusion.5), kind=kOutput, calls=%fused_computation.12.clone.1 | convolution fusion | flops 860095552 | bytes 26214528 | tf_op jit(solution)/shard_map/while/body/eval_jaxpr/bx,bjh->xjh/dot_general | solution.py:117
  481.1 12.8 %select_add_fusion.6 = f32[34,128,512]{2,0,1:T(8,128)S(1)} fusion(f32[34,128,512]{2,0,1:T(8,128)S(1)} %copy-done, pred[]{:T(512)S(6)} %compare.7, f32[32,128,512]{2,1,0:T(8,128)S(1)} %fusion.100, s32[32]{0:T(128)S(1)} %dynamic-slice_bitcast_fusion.5), kind=kOutput, calls=%fused_computation.12.clone.1 | convolution fusion | flops 860095552 | bytes 26214528 | tf_op jit(solution)/shard_map/while/body/eval_jaxpr/bx,bjh->xjh/dot_general | solution.py:117
  503.5 12.8 %select_add_fusion.6 = f32[34,128,512]{2,0,1:T(8,128)S(1)} fusion(f32[34,128,512]{2,0,1:T(8,128)S(1)} %copy-done, pred[]{:T(512)S(6)} %compare.7, f32[32,128,512]{2,1,0:T(8,128)S(1)} %fusion.100, s32[32]{0:T(128)S(1)} %dynamic-slice_bitcast_fusion.5), kind=kOutput, calls=%fused_computation.12.clone.1 | convolution fusion | flops 860095552 | bytes 26214528 | tf_op jit(solution)/shard_map/while/body/eval_jaxpr/bx,bjh->xjh/dot_general | solution.py:117
  525.9 12.8 %select_add_fusion.6 = f32[34,128,512]{2,0,1:T(8,128)S(1)} fusion(f32[34,128,512]{2,0,1:T(8,128)S(1)} %copy-done, pred[]{:T(512)S(6)} %compare.7, f32[32,128,512]{2,1,0:T(8,128)S(1)} %fusion.100, s32[32]{0:T(128)S(1)} %dynamic-slice_bitcast_fusion.5), kind=kOutput, calls=%fused_computation.12.clone.1 | convolution fusion | flops 860095552 | bytes 26214528 | tf_op jit(solution)/shard_map/while/body/eval_jaxpr/bx,bjh->xjh/dot_general | solution.py:117
  548.3 12.8 %select_add_fusion.6 = f32[34,128,512]{2,0,1:T(8,128)S(1)} fusion(f32[34,128,512]{2,0,1:T(8,128)S(1)} %copy-done, pred[]{:T(512)S(6)} %compare.7, f32[32,128,512]{2,1,0:T(8,128)S(1)} %fusion.100, s32[32]{0:T(128)S(1)} %dynamic-slice_bitcast_fusion.5), kind=kOutput, calls=%fused_computation.12.clone.1 | convolution fusion | flops 860095552 | bytes 26214528 | tf_op jit(solution)/shard_map/while/body/eval_jaxpr/bx,bjh->xjh/dot_general | solution.py:117
  570.7 12.8 %select_add_fusion.6 = f32[34,128,512]{2,0,1:T(8,128)S(1)} fusion(f32[34,128,512]{2,0,1:T(8,128)S(1)} %copy-done, pred[]{:T(512)S(6)} %compare.7, f32[32,128,512]{2,1,0:T(8,128)S(1)} %fusion.100, s32[32]{0:T(128)S(1)} %dynamic-slice_bitcast_fusion.5), kind=kOutput, calls=%fused_computation.12.clone.1 | convolution fusion | flops 860095552 | bytes 26214528 | tf_op jit(solution)/shard_map/while/body/eval_jaxpr/bx,bjh->xjh/dot_general | solution.py:117
  593.1 12.8 %select_add_fusion.6 = f32[34,128,512]{2,0,1:T(8,128)S(1)} fusion(f32[34,128,512]{2,0,1:T(8,128)S(1)} %copy-done, pred[]{:T(512)S(6)} %compare.7, f32[32,128,512]{2,1,0:T(8,128)S(1)} %fusion.100, s32[32]{0:T(128)S(1)} %dynamic-slice_bitcast_fusion.5), kind=kOutput, calls=%fused_computation.12.clone.1 | convolution fusion | flops 860095552 | bytes 26214528 | tf_op jit(solution)/shard_map/while/body/eval_jaxpr/bx,bjh->xjh/dot_general | solution.py:117
  615.5 12.8 %select_add_fusion.6 = f32[34,128,512]{2,0,1:T(8,128)S(1)} fusion(f32[34,128,512]{2,0,1:T(8,128)S(1)} %copy-done, pred[]{:T(512)S(6)} %compare.7, f32[32,128,512]{2,1,0:T(8,128)S(1)} %fusion.100, s32[32]{0:T(128)S(1)} %dynamic-slice_bitcast_fusion.5), kind=kOutput, calls=%fused_computation.12.clone.1 | convolution fusion | flops 860095552 | bytes 26214528 | tf_op jit(solution)/shard_map/while/body/eval_jaxpr/bx,bjh->xjh/dot_general | solution.py:117
  632.5 9.1 %copy.38 = f32[34,128,512]{2,1,0:T(8,128)S(1)} copy(f32[34,128,512]{2,0,1:T(8,128)} %get-tuple-element.204) | data formatting | bytes 17825792 | tf_op jit(solution)/shard_map/while | solution.py:122
  657.4 7.8 fusion.36
  667.5 7.5 fusion.28
  675.0 6.2 convolution_bitcast_fusion
  682.8 8.9 pad_maximum_fusion.1
  716.8 124.0 %all-reduce.3.cloned.1.call-done = f32[1377792]{0:T(1024)} async-done(((f32[1377792]{0:T(1024)}), f32[1377792]{0:T(1024)}) %all-reduce.3.cloned.1.call-update) | async-done | bytes 5511184 | tf_op jit(solution)/shard_map/psum | solution.py:219
  845.5 14.0 %multiply_subtract_fusion = (f32[1377792]{0:T(1024)S(1)}, f32[1377792]{0:T(1024)}, f32[1377792]{0:T(1024)S(1)}) fusion(f32[1377792]{0:T(1024)} %constant_dynamic-update-slice_fusion, f32[1377792]{0:T(1024)} %all-reduce.3.cloned.1.call-done, f32[]{:T(128)S(6)} %div.42, f32[20992]{0:T(1024)S(1)} %reshape.185, f32[524288]{0:T(1024)} %bitcast.103, ...), kind=kLoop, calls=%fused_computation.52 | loop fusion | flops 30311424 | bytes 38578180 | tf_op jit(solution)/shard_map/sub | solution.py:25
  (286 shorter events, 331.3 us)
Async XLA Ops:
  8.0 6.3 copy-start.29
  16.3 12.0 %copy-start.5 = (f32[1,2,512,512]{3,2,1,0:T(8,128)S(1)}, f32[1,2,512,512]{3,2,1,0:T(8,128)}, u32[]{:S(2)}) copy-start(f32[1,2,512,512]{3,2,1,0:T(8,128)} %param.29) | copy-start | bytes 6291460
  18.3 18.7 %all-to-all-start = ((bf16[32,8,512]{2,1,0:T(8,128)(2,1)}), bf16[32,8,512]{2,1,0:T(8,128)(2,1)}, u32[]{:S(2)}, u32[]{:S(2)}) async-start(bf16[32,8,512]{2,1,0:T(8,128)(2,1)} %fusion.53), calls=%async_computation | async-start | bytes 524288 | tf_op jit(solution)/shard_map/all_to_all | solution.py:54
  41.9 7.1 copy-start.2
  59.8 7.0 copy-start.2
  77.7 7.0 copy-start.2
  95.6 7.0 copy-start.2
  113.6 7.0 copy-start.2
  131.5 7.0 copy-start.2
  149.4 7.0 copy-start.2
  167.3 7.0 copy-start.2
  185.2 7.0 copy-start.2
  203.1 7.0 copy-start.2
  221.0 7.0 copy-start.2
  238.9 7.0 copy-start.2
  266.1 7.3 copy-start.33
  266.1 7.3 copy-start.23
  319.2 12.7 %slice-start.2 = ((s8[8388608]{0:T(1024)(128)(4,1)}), s8[4194304]{0:T(1024)(128)(4,1)S(1)}, s32[]{:S(2)}) async-start(s8[8388608]{0:T(1024)(128)(4,1)} %bitcast.101), calls=%async_computation.5 | async-start | bytes 8388608
  325.9 6.0 slice-start.3
  331.9 7.1 copy-start.32
  331.9 7.1 copy-start.34
  339.0 5.9 copy-start.18
  350.0 8.7 copy-start.15
  350.1 5.3 copy-start.14
  363.5 5.5 copy-start
  385.9 5.5 copy-start
  408.3 5.5 copy-start
  430.7 5.5 copy-start
  453.1 5.5 copy-start
  475.5 5.5 copy-start
  497.9 5.5 copy-start
  520.3 5.5 copy-start
  542.7 5.5 copy-start
  565.2 5.5 copy-start
  587.6 5.5 copy-start
  610.0 5.5 copy-start
  652.7 14.8 %all-to-all-start.1 = ((bf16[32,8,512]{2,1,0:T(8,128)(2,1)}), bf16[32,8,512]{2,1,0:T(8,128)(2,1)S(1)}, u32[]{:S(2)}, u32[]{:S(2)}) async-start(bf16[32,8,512]{2,1,0:T(8,128)(2,1)} %bitcast.120), calls=%async_computation.1 | async-start | bytes 524288 | tf_op jit(solution)/shard_map/all_to_all | solution.py:58
  657.3 10.2 %copy-start.30 = (s32[256]{0:T(256)S(1)}, s32[256]{0:T(256)}, u32[]{:S(2)}) copy-start(s32[256]{0:T(256)} %copy-done.29) | copy-start | bytes 3076
  657.3 183.5 %all-reduce.3.cloned.1.call-start = ((), (), s32[]{:S(2)}) async-start(), calls=%async_computation.2 | async-start | bytes 11026432 | tf_op jit(solution)/shard_map/psum | solution.py:219
  691.7 6.6 copy-start.25
  694.7 9.1 %copy-start.19 = (f32[1,2,512,512]{3,2,1,0:T(8,128)S(1)}, f32[1,2,512,512]{3,2,1,0:T(8,128)}, u32[]{:S(2)}) copy-start(f32[1,2,512,512]{3,2,1,0:T(8,128)} %param.33) | copy-start | bytes 6291460
  694.7 11.0 %copy-start.21 = (f32[602,512]{1,0:T(8,128)S(1)}, f32[602,512]{1,0:T(8,128)}, u32[]{:S(2)}) copy-start(f32[602,512]{1,0:T(8,128)} %param.32) | copy-start | bytes 3698692
  700.3 6.5 copy-start.26
  705.7 6.6 copy-start.20
  706.8 7.4 copy-start.22
  872.4 9.3 %copy-start.8 = (f32[524288]{0:T(1024)S(1)}, f32[524288]{0:T(1024)}, u32[]{:S(2)}) copy-start(f32[524288]{0:T(1024)} %get-tuple-element.305) | copy-start | bytes 6291460
  879.2 9.6 %copy-start.9 = (f32[308224]{0:T(1024)S(1)}, f32[308224]{0:T(1024)}, u32[]{:S(2)}) copy-start(f32[308224]{0:T(1024)} %slice.129) | copy-start | bytes 3698692
  883.2 9.5 %copy-start.7 = (f32[524288]{0:T(1024)S(1)}, f32[524288]{0:T(1024)}, u32[]{:S(2)}) copy-start(f32[524288]{0:T(1024)} %get-tuple-element.293) | copy-start | bytes 6291460
  (38 other events, 130.8 us)
Sparse Core Ops, SparseCore 0:
  691.8 148.9 all-reduce.2
where the time goes:
time: 912 us; the launch traced here: 904 us
  matrix products  449 us (49%)
  local copies, waits for them, and re-layouts  211 us (23%)
  waiting for transfers between devices  126 us (14%)
  other arithmetic  46 us (5%)
  blocking collectives  40.7 us (4%)
  between operations  16.9 us (2%)
  starting transfers between devices  12.1 us (1%)
    dot_general x12, matrix products, add_tile(): jnp.einsum('bx,bjh->xjh', choose, term, precision=HIGHEST, preferred_elem...  154 us
    psum x1, waiting for transfers between devices, shards(): summed = lax.psum(flat_grad, ('wide', 'narrow'))  124 us
    while x96, local copies, waits for them, and re-layouts  91.2 us
    dot_general x12, matrix products, add_tile(): jnp.einsum('bij,bjh->bih', weights_now, selected, preferred_element_type=...  90.9 us
    dot_general x12, matrix products, add_tile(): jnp.einsum('bx,xjh->bjh', choose, extended, preferred_element_type=jnp.fl...  74.3 us
    dot_general x12, matrix products, add_tile(): jnp.einsum('bij,bih->bjh', weights_now, grad_agg, preferred_element_type=...  47.4 us
    psum x1, blocking collectives, shards(): lax.psum((local_loss, jnp.sum(mask_vals)), ('wide', 'narrow'))  40.7 us
    unnamed x88, local copies, waits for them, and re-layouts  37.1 us
  transfers between devices with their start and end apart: 3, of which 2 were waited for; matrix products, arithmetic and copies ran while one was open for 5% of the time, Pallas kernels for 0%

commit v1 on v0

v1 whole, which is shorter than its diff:
```python
import functools

import jax
import jax.numpy as jnp
from jax import lax
from jax.experimental import pallas as pl
from jax.experimental.pallas import tpu as pltpu
from jax.sharding import PartitionSpec as P

ADAM_STEP = 10
NORM_EPS = 1e-06
SMOOTHING = 0.1
CLIP_AT = 0.002
LEARN_RATE = 0.05
BETA_FIRST = 0.9
BETA_SECOND = 0.999
ADAM_EPS = 1e-08
WEIGHT_DECAY = 0.01

AXES = ("wide", "narrow")
LANES = 128
TAIL = 8
GELU_A = 0.7978845608028654
GELU_B = 0.044715
F32 = jnp.float32
BF16 = jnp.bfloat16
VMEM_LIMIT = 58 * 1024 * 1024


def mm(left, right):
    return jnp.dot(left, right, preferred_element_type=F32)


def mm_nt(left, right):
    return lax.dot_general(left, right, (((1,), (1,)), ((), ())), preferred_element_type=F32)


def mm_tn(left, right):
    return lax.dot_general(left, right, (((0,), (0,)), ((), ())), preferred_element_type=F32)


def split_tail(rows, is_last):
    tail = rows[-TAIL:]
    total = tail + pltpu.roll(tail, TAIL - 1, 0)
    high = total.astype(BF16).astype(F32)
    low = pltpu.roll(total - high, 1, 0)
    even = lax.broadcasted_iota(jnp.int32, tail.shape, 0) % 2 == 0
    tail = jnp.where(is_last, jnp.where(even, high, low), tail)
    return jnp.concatenate([rows[:-TAIL], tail], axis=0).astype(BF16)


def weights_kernel(w_in, w_pair, w_cat, w_out, big, prod, in_t, pair_t, cat_b, out_b):
    fan_in, hidden = w_in.shape
    padded = big.shape[0] // 2
    classes = w_out.shape[1]
    in_b = jnp.concatenate(
        [w_in[...].astype(BF16), jnp.zeros((padded - fan_in, hidden), BF16)], axis=0
    )
    in_t[...] = in_b.T
    cat_b[...] = w_cat[...].astype(BF16)
    out_b[...] = jnp.concatenate(
        [w_out[...].astype(BF16), jnp.zeros((hidden, LANES - classes), BF16)], axis=1
    )
    for side in range(2):
        pair_b = w_pair[side].astype(BF16)
        pair_t[side] = pair_b.T
        both = mm(pair_b, cat_b[side * hidden : (side + 1) * hidden, :]).astype(BF16)
        prod[side] = both
        big[side * padded : (side + 1) * padded, :] = mm(in_b, both).astype(BF16)


def weight_products(w_in, w_pair, w_cat, w_out, padded):
    hidden = w_in.shape[1]
    shapes = (
        (2 * padded, hidden),
        (2, hidden, hidden),
        (hidden, padded),
        (2, hidden, hidden),
        (2 * hidden, hidden),
        (hidden, LANES),
    )
    return pl.pallas_call(
        weights_kernel,
        out_shape=[jax.ShapeDtypeStruct(s, BF16) for s in shapes],
        compiler_params=pltpu.CompilerParams(vmem_limit_bytes=VMEM_LIMIT),
        cost_estimate=pl.CostEstimate(
            flops=4 * hidden * hidden * (hidden + padded),
            bytes_accessed=12 * 1024 * 1024,
            transcendentals=0,
        ),
        name="weight_products",
    )(w_in, w_pair, w_cat, w_out)


def nodes_kernel(
    geometry,
    src,
    me,
    feat,
    halo,
    edge,
    labels,
    mask,
    big,
    out_b,
    keep,
    send,
    ext,
    acc,
    acc_out,
    acc_loss,
):
    fan_in, classes, steps = geometry
    nb, tile, padded = ext.shape[0] - halo.shape[0] // ext.shape[1], ext.shape[1], ext.shape[2]
    per_step, kt = edge.shape[0], edge.shape[1]
    rows = per_step * tile
    hidden = big.shape[1]
    step = pl.program_id(0)

    @pl.when(step == 0)
    def _():
        zeros = jnp.zeros((tile, padded - fan_in), BF16)

        def fill(block, carry):
            own = feat[pl.ds(pl.multiple_of(block * tile, tile), tile), :]
            ext[block] = jnp.concatenate([own, zeros], axis=1)
            return carry

        lax.fori_loop(0, nb, fill, 0)
        for block in range(halo.shape[0] // tile):
            ext[nb + block] = halo[block * tile : (block + 1) * tile, :]
        acc[...] = jnp.zeros_like(acc)
        acc_out[...] = jnp.zeros_like(acc_out)
        acc_loss[...] = jnp.zeros_like(acc_loss)

    sums = []
    for j in range(per_step):
        block = step * per_step + j
        gathered = jnp.concatenate([ext[src[block * kt + k]] for k in range(kt)], axis=0)
        weights = jnp.concatenate([edge[j, k] for k in range(kt)], axis=1)
        sums.append(mm(weights, gathered).astype(BF16))
    own = ext[pl.ds(step * per_step, per_step)].reshape(rows, padded)
    both = jnp.concatenate([own, jnp.concatenate(sums, axis=0)], axis=1)
    mixed = mm(both, big[...])
    square = mixed * mixed
    curve = jnp.tanh(mixed * (GELU_A + (GELU_A * GELU_B) * square))
    half = 0.5 + 0.5 * curve
    active = mixed * half
    slope = half + (0.5 * mixed) * (1.0 - curve * curve) * (
        GELU_A + (3.0 * GELU_A * GELU_B) * square
    )
    inverse = lax.rsqrt(jnp.sum(active * active, axis=1, keepdims=True) / hidden + NORM_EPS)
    top = (active * inverse).astype(BF16)
    logits = mm(top, out_b[...])
    lane = lax.broadcasted_iota(jnp.int32, (rows, LANES), 1)
    logits = jnp.where(lane < classes, logits, -1e30)
    logits = logits - jnp.max(logits, axis=1, keepdims=True)
    powers = jnp.exp(logits)
    total = jnp.sum(powers, axis=1, keepdims=True)
    sub = lax.broadcasted_iota(jnp.int32, (LANES, tile), 0)
    turned = []
    for j in range(per_step):
        block = step * per_step + j
        hot = (sub == labels[pl.ds(block, 1), :]).astype(F32)
        hot = jnp.where(sub == LANES - 1, mask[pl.ds(block, 1), :].astype(F32), hot)
        turned.append(hot.T)
    turned = jnp.concatenate(turned, axis=0)
    used = turned[:, LANES - 1 :]
    target = jnp.where(
        lane < classes, (1.0 - SMOOTHING) * turned + SMOOTHING / classes, 0.0
    )
    loss = -(target * (logits - jnp.log(total))) * used
    acc_loss[0:1, :] += jnp.sum(loss, axis=0, keepdims=True)
    acc_loss[1:2, :] += jnp.sum(jnp.where(lane == 0, used, 0.0), axis=0, keepdims=True)
    grad_logits = ((powers / total - target) * used).astype(BF16)
    acc_out[...] += mm_tn(grad_logits, top)
    grad_top = mm_nt(grad_logits, out_b[...])
    along = jnp.sum(active * grad_top, axis=1, keepdims=True)
    pull = inverse * inverse * inverse * along / hidden
    grad_mixed = ((inverse * grad_top - active * pull) * slope).astype(BF16)
    acc[...] += mm_tn(both, grad_mixed)

    @pl.when(step == steps - 1)
    def _():
        first = padded - fan_in
        acc[fan_in:padded, :] = acc_out[:first, :]
        acc[padded + fan_in : padded + fan_in + classes - first, :] = acc_out[first:classes, :]
        row = lax.broadcasted_iota(jnp.int32, (TAIL, hidden), 0)
        loss_sum = jnp.sum(acc_loss[0:1, :])
        count = jnp.sum(acc_loss[1:2, :])
        tail = jnp.where(row == 0, loss_sum, jnp.where(row == 2, count, 0.0))
        acc[2 * padded - TAIL :, :] = tail
        core = me[0]
        pieces, piece = keep.shape[0], keep.shape[1]
        for p in range(pieces):
            mine = pl.multiple_of(core * padded + p * piece, TAIL)
            other = pl.multiple_of((1 - core) * padded + p * piece, TAIL)
            keep[p] = acc[pl.ds(mine, piece), :]
            is_last = jnp.logical_and(core == 0, p == pieces - 1)
            send[p] = split_tail(acc[pl.ds(other, piece), :], is_last)


def node_pass(src, me, feat, halo, edge, labels, mask, big, out_b, classes, pieces):
    nodes, fan_in = feat.shape
    nb, kt, tile, _ = edge.shape
    padded = halo.shape[1]
    hidden = big.shape[1]
    per_step = 4
    steps = nb // per_step
    piece = padded // pieces
    once = pl.Buffered(buffer_count=1)
    full = lambda shape: pl.BlockSpec(shape, lambda i, *_: (0,) * len(shape), pipeline_mode=once)
    out_full = lambda shape: pl.BlockSpec(shape, lambda i, *_: (0,) * len(shape))
    return pl.pallas_call(
        functools.partial(nodes_kernel, (fan_in, classes, steps)),
        out_shape=[
            jax.ShapeDtypeStruct((pieces, piece, hidden), F32),
            jax.ShapeDtypeStruct((pieces, piece, hidden), BF16),
        ],
        grid_spec=pltpu.PrefetchScalarGridSpec(
            num_scalar_prefetch=2,
            grid=(steps,),
            in_specs=[
                full((nodes, fan_in)),
                full(halo.shape),
                pl.BlockSpec((per_step, kt, tile, tile), lambda i, *_: (i, 0, 0, 0)),
                full(labels.shape),
                full(mask.shape),
                full(big.shape),
                full(out_b.shape),
            ],
            out_specs=[out_full((pieces, piece, hidden))] * 2,
            scratch_shapes=[
                pltpu.VMEM((nb + halo.shape[0] // tile, tile, padded), BF16),
                pltpu.VMEM((2 * padded, hidden), F32),
                pltpu.VMEM((LANES, hidden), F32),
                pltpu.VMEM((TAIL, LANES), F32),
            ],
        ),
        compiler_params=pltpu.CompilerParams(
            vmem_limit_bytes=VMEM_LIMIT, dimension_semantics=("arbitrary",)
        ),
        name="node_pass",
    )(src, me, feat, halo, edge, labels, mask, big, out_b)


def pair_sum_kernel(me, keep, got, own, *outs):
    pieces = keep.shape[0]
    core, plane = me[0], me[1]
    own[...] = keep[plane] + got[plane].astype(F32)
    for d in range(1, pieces):
        p = plane ^ d
        total = keep[p] + got[p].astype(F32)
        outs[d - 1][...] = split_tail(total, jnp.logical_and(core == 1, p == pieces - 1))


def plane_sum_kernel(pieces, me, own, *refs):
    total = own[...]
    for ref in refs[:-1]:
        total = total + ref[...].astype(F32)
    is_last = jnp.logical_and(me[0] == 1, me[1] == pieces - 1)
    refs[-1][...] = split_tail(total, is_last)


def line_sum_kernel(pieces, me, *refs):
    parts = [ref[...].astype(F32) for ref in refs[:-1]]
    while len(parts) > 1:
        parts = [parts[i] + parts[i + 1] for i in range(0, len(parts), 2)]
    is_last = jnp.logical_and(me[0] == 1, me[1] == pieces - 1)
    refs[-1][...] = split_tail(parts[0], is_last)


def small_call(kernel, me, operands, shapes, name):
    spec = pl.BlockSpec(memory_space=pltpu.VMEM)
    return pl.pallas_call(
        kernel,
        out_shape=shapes,
        in_specs=[pl.BlockSpec(memory_space=pltpu.SMEM)] + [spec] * len(operands),
        out_specs=[spec] * len(shapes),
        compiler_params=pltpu.CompilerParams(vmem_limit_bytes=VMEM_LIMIT),
        name=name,
    )(me, *operands)


def update_kernel(geometry, me, *refs):
    fan_in, classes, pieces = geometry
    got = refs[: 2 * pieces]
    prod, in_t, pair_t, cat_b = refs[2 * pieces : 2 * pieces + 4]
    states = refs[2 * pieces + 4 : 2 * pieces + 16]
    news = refs[2 * pieces + 16 : 2 * pieces + 28]
    loss_out, count_out, norm_out = refs[2 * pieces + 28 : 2 * pieces + 31]
    rest = refs[2 * pieces + 31 :]
    bufs = rest[:12]
    summed, g_in, g_pair, g_cat, g_out, sems_in, sems_out = rest[12:]
    hidden = prod.shape[1]
    padded = in_t.shape[1]
    core, plane = me[0], me[1]
    loads = [pltpu.make_async_copy(states[n], bufs[n], sems_in.at[n]) for n in range(12)]
    for load in loads:
        load.start()
    piece = padded // pieces
    for d in range(pieces):
        at = (plane ^ d) * piece
        mine = pl.multiple_of(core * padded + at, TAIL)
        other = pl.multiple_of((1 - core) * padded + at, TAIL)
        summed[pl.ds(mine, piece), :] = got[d][...].astype(F32)
        summed[pl.ds(other, piece), :] = got[pieces + d][...].astype(F32)
    first = padded - fan_in
    tail = summed[2 * padded - TAIL :, :]
    loss_sum = jnp.max(tail[0:1, :] + tail[1:2, :])
    count = jnp.max(tail[2:3, :] + tail[3:4, :])
    top = jnp.concatenate(
        [
            summed[fan_in:padded, :],
            summed[padded + fan_in : padded + fan_in + classes - first, :],
            jnp.zeros((LANES - classes, hidden), F32),
        ],
        axis=0,
    )
    g_out[...] = top.T[:, :classes]
    squares = jnp.sum(top * top)
    both = [summed[s * padded : (s + 1) * padded, :].astype(BF16) for s in range(2)]
    grad = mm_nt(both[0], prod[0]) + mm_nt(both[1], prod[1])
    grad = grad[:fan_in, :]
    g_in[...] = grad
    squares += jnp.sum(grad * grad)
    for side in range(2):
        inner = mm(in_t[...], both[side]).astype(BF16)
        grad = mm_nt(inner, cat_b[side * hidden : (side + 1) * hidden, :])
        g_pair[0, side] = grad
        squares += jnp.sum(grad * grad)
        grad = mm(pair_t[side], inner)
        g_cat[0, side * hidden : (side + 1) * hidden, :] = grad
        squares += jnp.sum(grad * grad)
    norm = jnp.sqrt(squares) / count
    factor = (CLIP_AT / jnp.maximum(norm, CLIP_AT)) / count
    loss_out[0] = loss_sum
    count_out[0] = count
    norm_out[0] = norm
    stores = []
    for n, grads in enumerate((g_in, g_pair, g_cat, g_out)):
        w, m, v = bufs[n], bufs[4 + n], bufs[8 + n]
        for k in range(3):
            loads[4 * k + n].wait()
        grad = grads[...] * factor
        first_new = BETA_FIRST * m[...] + (1.0 - BETA_FIRST) * grad
        second_new = BETA_SECOND * v[...] + (1.0 - BETA_SECOND) * grad * grad
        m[...] = first_new
        v[...] = second_new
        first_hat = first_new / (1.0 - BETA_FIRST**ADAM_STEP)
        second_hat = second_new / (1.0 - BETA_SECOND**ADAM_STEP)
        w[...] = w[...] - LEARN_RATE * (
            first_hat / (jnp.sqrt(second_hat) + ADAM_EPS) + WEIGHT_DECAY * w[...]
        )
        for k in range(3):
            store = pltpu.make_async_copy(bufs[4 * k + n], news[4 * k + n], sems_out.at[4 * k + n])
            store.start()
            stores.append(store)
    for store in stores:
        store.wait()


def update(me, got, matrices, states, classes):
    fan_in, hidden = states[0].shape
    padded = matrices[1].shape[1]
    pieces = len(got) // 2
    vmem = pl.BlockSpec(memory_space=pltpu.VMEM)
    smem = pl.BlockSpec(memory_space=pltpu.SMEM)
    hbm = pl.BlockSpec(memory_space=pl.ANY)
    shapes = [jax.ShapeDtypeStruct(s.shape, F32) for s in states]
    return pl.pallas_call(
        functools.partial(update_kernel, (fan_in, classes, pieces)),
        out_shape=shapes + [jax.ShapeDtypeStruct((1,), F32)] * 3,
        in_specs=[smem] + [vmem] * (len(got) + 4) + [hbm] * 12,
        out_specs=[hbm] * 12 + [smem] * 3,
        scratch_shapes=[pltpu.VMEM(s.shape, F32) for s in states]
        + [pltpu.VMEM((2 * padded, hidden), F32)]
        + [pltpu.VMEM(s.shape, F32) for s in states[:4]]
        + [pltpu.SemaphoreType.DMA((12,)), pltpu.SemaphoreType.DMA((12,))],
        compiler_params=pltpu.CompilerParams(vmem_limit_bytes=VMEM_LIMIT),
        name="update",
    )(me, *got, *matrices, *states)


def shards(wide_count, narrow_count, *args):
    features, tile_src, edge_weight, send_lists, labels, train_mask = args[:6]
    states = args[6:18]
    w_in, w_pair, w_cat, w_out = states[:4]
    nodes, fan_in = features.shape
    nb, kt, tile, _ = edge_weight.shape
    classes = w_out.shape[1]
    hidden = w_in.shape[1]
    padded = -(-fan_in // LANES) * LANES
    pieces = wide_count // 2
    piece = padded // pieces
    wide = lax.axis_index("wide")
    me = jnp.stack([wide % 2, wide // 2]).astype(jnp.int32)

    def swap(value, wide_bits, narrow_bits):
        pairs = [
            (w * narrow_count + n, (w ^ wide_bits) * narrow_count + (n ^ narrow_bits))
            for w in range(wide_count)
            for n in range(narrow_count)
        ]
        return lax.ppermute(value, AXES, pairs)

    slots = send_lists.reshape(-1)
    picker = (slots[:, None] == jnp.arange(nodes, dtype=jnp.int32)[None, :]).astype(BF16)
    outgoing = mm(picker, features).astype(BF16)
    outgoing = jnp.pad(outgoing, ((0, 0), (0, padded - fan_in)))
    outgoing = outgoing.reshape(send_lists.shape[1], send_lists.shape[2], padded)
    halo = lax.all_to_all(outgoing, AXES, split_axis=0, concat_axis=0, tiled=True)
    halo = halo.reshape(-1, padded)

    big, prod, in_t, pair_t, cat_b, out_b = weight_products(
        w_in, w_pair[0], w_cat[0], w_out, padded
    )
    keep, send = node_pass(
        tile_src.reshape(-1),
        me,
        features,
        halo,
        edge_weight,
        labels.reshape(nb, tile),
        train_mask.reshape(nb, tile),
        big,
        out_b,
        classes,
        pieces,
    )
    part_b = jax.ShapeDtypeStruct((piece, hidden), BF16)
    part_f = jax.ShapeDtypeStruct((piece, hidden), F32)
    got = swap(send, 1, 0)
    own, *outs = small_call(
        pair_sum_kernel, me, (keep, got), [part_f] + [part_b] * (pieces - 1), "pair_sum"
    )
    got = [swap(outs[d - 1], 2 * d, 0) for d in range(1, pieces)]
    (own,) = small_call(
        functools.partial(plane_sum_kernel, pieces), me, (own, *got), [part_b], "plane_sum"
    )
    got = [swap(own, 0, d) for d in range(1, narrow_count)]
    (own,) = small_call(
        functools.partial(line_sum_kernel, pieces), me, (own, *got), [part_b], "line_sum"
    )
    mine = [own] + [swap(own, 2 * d, 0) for d in range(1, pieces)]
    other = [swap(part, 1, 0) for part in mine]
    results = update(me, mine + other, (prod, in_t, pair_t, cat_b), states, classes)
    return tuple(results[:12]) + tuple(r.reshape(()) for r in results[12:])


def solution(mesh):
    split = P(("wide", "narrow"))
    in_specs = (split,) * 6 + (P(),) * 12
    out_specs = (P(),) * 15
    body = functools.partial(shards, mesh.shape["wide"], mesh.shape["narrow"])
    return jax.shard_map(body, mesh=mesh, in_specs=in_specs, out_specs=out_specs, check_vma=False)
```

time: 912 us -> 146 us (0.16)
  matrix products: 449 us -> 4.06 us
  local copies, waits for them, and re-layouts: 211 us -> 22.4 us
  waiting for transfers between devices: 126 us -> 28.7 us
  Pallas kernels: 0 us -> 68.8 us
  other arithmetic: 46 us -> 0.58 us
  blocking collectives: 40.7 us -> 0 us
  between operations: 16.9 us -> 0.83 us
    dot_general x64 -> x1, matrix products: 449 us -> 4.06 us  [mm(): return jnp.dot(left, right, preferred_element_type=F32)]
    psum x1 -> x0, waiting for transfers between devices: 124 us -> none  [shards(): summed = lax.psum(flat_grad, ('wide', 'narrow'))]
    while x97 -> x0, local copies, waits for them, and re-layouts: 100 us -> none
    pallas_call x0 -> x6, Pallas kernels: none -> 68.8 us  [the longest x1 41.1 us: node_pass(): pl.pallas_call(functools.partial(nodes_kernel, (fan_in, classes, steps)),...]
    psum x1 -> x0, blocking collectives: 40.7 us -> none  [shards(): lax.psum((local_loss, jnp.sum(mask_vals)), ('wide', 'narrow'))]
    ppermute x0 -> x14, waiting for transfers between devices: none -> 28.7 us  [swap(): return lax.ppermute(value, AXES, pairs)]
    eq x25 -> x1, local copies, waits for them, and re-layouts: 25.5 us -> 0.09 us  [shards(): slots[:, None] == jnp.arange(nodes, dtype=jnp.int32)[None, :]]
    reshape x17 -> x2, local copies, waits for them, and re-layouts: 26.2 us -> 1.44 us  [the longest x1 0.76 us: shards(): outgoing.reshape(send_lists.shape[1], send_lists.shape[2], padded)]
  transfers between devices with their start and end apart: 3 -> 15, of which waited for: 2 -> 7; matrix products, arithmetic and copies ran while one was open for 5% -> 8% of each run, Pallas kernels for 0% -> 4%
where the time goes in v1:
time: 146 us; the launch traced here: 145 us
  Pallas kernels  68.8 us (47%)
  waiting for transfers between devices  28.7 us (20%)
  local copies, waits for them, and re-layouts  22.4 us (15%)
  starting transfers between devices  19.5 us (13%)
  matrix products  4.06 us (3%)
    pallas_call x1, Pallas kernels, node_pass(): pl.pallas_call(functools.partial(nodes_kernel, (fan_in, classes, steps)),...  41.1 us
    ppermute x14, waiting for transfers between devices, swap(): return lax.ppermute(value, AXES, pairs)  28.7 us
    unnamed x48, local copies, waits for them, and re-layouts  20.9 us
    pallas_call x1, Pallas kernels, update(): pl.pallas_call(functools.partial(update_kernel, (fan_in, classes, pieces)...  15.4 us
    ppermute x14, starting transfers between devices, swap(): return lax.ppermute(value, AXES, pairs)  12.2 us
    all_to_all x1, starting transfers between devices, shards(): lax.all_to_all(outgoing, AXES, split_axis=0, concat_axis=0, tiled=True)  7.3 us
    pallas_call x3, Pallas kernels, small_call(): pl.pallas_call(kernel, out_shape=shapes, in_specs=[pl.BlockSpec(memory_sp...  6.31 us
    pallas_call x1, Pallas kernels, weight_products(): pl.pallas_call(weights_kernel, out_shape=[jax.ShapeDtypeStruct(s, BF16) f...  6.11 us
  transfers between devices with their start and end apart: 15, of which 7 were waited for; matrix products, arithmetic and copies ran while one was open for 8% of the time, Pallas kernels for 4%

profile of v1, /device:TPU:0, one launch (start us, length us, event | category | flops | bytes accessed | tf_op | source)
XLA Modules:
  0.0 145.0 jit_solution(11023505570894930459)
XLA Ops:
  0.6 0.8 copy.43
  1.4 0.1 eq.17
  1.5 4.1 %fusion.2 = bf16[256,602]{0,1:T(8,128)(2,1)S(1)} fusion(bf16[4096,602]{0,1:T(8,128)(2,1)} %param.18, s32[256]{0:T(256)S(1)} %eq.17), kind=kOutput, calls=%fused_computation.3 | convolution fusion | flops 1263688192 | bytes 5240832 | tf_op jit(solution)/shard_map/dot_general | solution.py:31
  5.6 0.2 copy.53
  5.8 0.8 pad_bitcast_fusion
  6.5 7.3 %all-to-all-start = ((bf16[32,8,640]{2,1,0:T(8,128)(2,1)}), bf16[32,8,640]{2,1,0:T(8,128)(2,1)S(1)}, u32[]{:S(2)}, u32[]{:S(2)}) async-start(bf16[32,8,640]{2,1,0:T(8,128)(2,1)} %pad_bitcast_fusion), calls=%async_computation | async-start | bytes 655360 | tf_op jit(solution)/shard_map/all_to_all | solution.py:412
  13.9 7.8 %copy.46.feat = bf16[4096,602]{1,0:T(8,128)(2,1)} copy(bf16[4096,602]{0,1:T(8,128)(2,1)} %param.18) | data formatting | bytes 9863168 | tf_op args[0]
  21.7 0.1 copy.42
  21.7 0.7 reshape.55.src
  22.4 0.8 copy.45.w_out.refs_15_
  23.3 0.6 pad_add_fusion.me
  23.9 6.1 %weight_products.1 = (bf16[1280,512]{1,0:T(8,128)(2,1)}, bf16[2,512,512]{2,1,0:T(8,128)(2,1)}, bf16[512,640]{1,0:T(8,128)(2,1)}, bf16[2,512,512]{2,1,0:T(8,128)(...) custom-call(f32[602,512]{1,0:T(8,128)} %refs_12_.1, f32[2,512,512]{2,1,0:T(8,128)} %bitcast.13, ...), custom_call_target="tpu_custom_call" | custom-call | flops 1207959552 | bytes 12582912 | tf_op jit(solution)/shard_map/weight_products/pallas_call | solution.py:82
  30.0 0.7 copy-done
  30.7 41.1 %node_pass.1 = (f32[4,160,512]{2,1,0:T(8,128)}, bf16[4,160,512]{2,1,0:T(8,128)(2,1)}) custom-call(s32[384]{0:T(512)} %reshape.55.src, s32[2]{0:T(128)} %pad_add_fusion.me, bf16[4096,602]{1,0:T(8,128)(2,1)} %copy.46.feat, bf16[256,640]{1,0:T(8,128)(2,1)} %bitcast.15, bf16[32,12,128,128]{3,2,1,0:T(8,128)(2,1)} %edge.1, s32[32,128]{1,0:T(8,128)} %bitcast.16, ...), custom_call_target="tpu_custom_call" | custom-call | tf_op jit(solution)/shard_map/node_pass/pallas_call | solution.py:214
  71.8 0.3 collective-permute-start
  72.1 2.1 %collective-permute-done.got = bf16[4,160,512]{2,1,0:T(8,128)(2,1)S(1)} collective-permute-done((bf16[4,160,512]{2,1,0:T(8,128)(2,1)}, bf16[4,160,512]{2,1,0:T(8,128)(2,1)S(1)}, u32[]{:S(2)}, u32[]{:S(2)}) %collective-permute-start) | collective-permute-done | bytes 655392 | tf_op jit(solution)/shard_map/ppermute | solution.py:405
  74.1 0.8 copy-done.1
  75.0 2.5 %pair_sum.1 = (f32[160,512]{1,0:T(8,128)}, bf16[160,512]{1,0:T(8,128)(2,1)}, bf16[160,512]{1,0:T(8,128)(2,1)}, bf16[160,512]{1,0:T(8,128)(2,1)}) custom-call(s32[2]{0:T(128)} %pad_add_fusion.me, f32[4,160,512]{2,1,0:T(8,128)} %get-tuple-element.44.keep, bf16[4,160,512]{2,1,0:T(8,128)(2,1)} %copy-done.1), custom_call_target="tpu_custom_call" | custom-call | tf_op jit(solution)/shard_map/pair_sum/pallas_call | solution.py:275
  77.4 1.8 %collective-permute-start.1 = (bf16[160,512]{1,0:T(8,128)(2,1)}, bf16[160,512]{1,0:T(8,128)(2,1)S(1)}, u32[]{:S(2)}, u32[]{:S(2)}) collective-permute-start(bf16[160,512]{1,0:T(8,128)(2,1)} %get-tuple-element.47), channel_id=1, source_target_pairs={{0,8},{1,9},{2,10},{3,11},{4,12},{5,13},{6,14},{7,15},{8,0},{9,1},... | collective-permute-start | bytes 491528 | tf_op jit(solution)/shard_map/ppermute | solution.py:405
  79.2 1.5 %collective-permute-start.2 = (bf16[160,512]{1,0:T(8,128)(2,1)}, bf16[160,512]{1,0:T(8,128)(2,1)S(1)}, u32[]{:S(2)}, u32[]{:S(2)}) collective-permute-start(bf16[160,512]{1,0:T(8,128)(2,1)} %get-tuple-element.48), channel_id=1, source_target_pairs={{0,16},{1,17},{2,18},{3,19},{4,20},{5,21},{6,22},{7,23},{8,24},{9,... | collective-permute-start | bytes 491528 | tf_op jit(solution)/shard_map/ppermute | solution.py:405
  80.7 0.3 collective-permute-start.3
  80.9 3.8 %collective-permute-done.1.refs_0_ = bf16[160,512]{1,0:T(8,128)(2,1)S(1)} collective-permute-done((bf16[160,512]{1,0:T(8,128)(2,1)}, bf16[160,512]{1,0:T(8,128)(2,1)S(1)}, u32[]{:S(2)}, u32[]{:S(2)}) %collective-permute-start.1) | collective-permute-done | bytes 163872 | tf_op jit(solution)/shard_map/ppermute | solution.py:405
  84.7 4.2 %collective-permute-done.2.refs_1_ = bf16[160,512]{1,0:T(8,128)(2,1)S(1)} collective-permute-done((bf16[160,512]{1,0:T(8,128)(2,1)}, bf16[160,512]{1,0:T(8,128)(2,1)S(1)}, u32[]{:S(2)}, u32[]{:S(2)}) %collective-permute-start.2) | collective-permute-done | bytes 163872 | tf_op jit(solution)/shard_map/ppermute | solution.py:405
  88.9 0.7 copy-done.10
  89.6 0.1 copy-done.11
  89.6 1.9 %plane_sum.1.refs_0_ = bf16[160,512]{1,0:T(8,128)(2,1)} custom-call(s32[2]{0:T(128)} %pad_add_fusion.me, f32[160,512]{1,0:T(8,128)} %get-tuple-element.46.own, bf16[160,512]{1,0:T(8,128)(2,1)} %copy-done.9, bf16[160,512]{1,0:T(8,128)(2,1)} %copy-done.10, bf16[160,512]{1,0:T(8,128)(2,1)} %copy-done.11), custom_call_target="tpu_custom_call" | custom-call | tf_op jit(solution)/shard_map/plane_sum/pallas_call | solution.py:275
  91.5 3.3 %collective-permute-start.6 = (bf16[160,512]{1,0:T(8,128)(2,1)}, bf16[160,512]{1,0:T(8,128)(2,1)S(1)}, u32[]{:S(2)}, u32[]{:S(2)}) collective-permute-start(bf16[160,512]{1,0:T(8,128)(2,1)} %plane_sum.1.refs_0_), channel_id=1, source_target_pairs={{0,3},{1,2},{2,1},{3,0},{4,7},{5,6},{6,5},{7,4},{8,11},{9,10},{10,... | collective-permute-start | bytes 491528 | tf_op jit(solution)/shard_map/ppermute | solution.py:405
  94.9 1.1 collective-permute-start.4
  95.9 4.8 %collective-permute-done.6.refs_3_ = bf16[160,512]{1,0:T(8,128)(2,1)S(1)} collective-permute-done((bf16[160,512]{1,0:T(8,128)(2,1)}, bf16[160,512]{1,0:T(8,128)(2,1)S(1)}, u32[]{:S(2)}, u32[]{:S(2)}) %collective-permute-start.6) | collective-permute-done | bytes 163872 | tf_op jit(solution)/shard_map/ppermute | solution.py:405
  100.7 7.6 %collective-permute-done.5.refs_2_ = bf16[160,512]{1,0:T(8,128)(2,1)S(1)} collective-permute-done((bf16[160,512]{1,0:T(8,128)(2,1)}, bf16[160,512]{1,0:T(8,128)(2,1)S(1)}, u32[]{:S(2)}, u32[]{:S(2)}) %collective-permute-start.5) | collective-permute-done | bytes 163872 | tf_op jit(solution)/shard_map/ppermute | solution.py:405
  108.3 0.7 copy-done.13
  109.0 0.7 copy-done.14
  109.7 1.9 %line_sum.1.refs_0_ = bf16[160,512]{1,0:T(8,128)(2,1)} custom-call(s32[2]{0:T(128)} %pad_add_fusion.me, bf16[160,512]{1,0:T(8,128)(2,1)} %plane_sum.1.refs_0_, bf16[160,512]{1,0:T(8,128)(2,1)} %copy-done.14, bf16[160,512]{1,0:T(8,128)(2,1)} %copy-done.13, bf16[160,512]{1,0:T(8,128)(2,1)} %copy-done.12), custom_call_target="tpu_custom_call" | custom-call | tf_op jit(solution)/shard_map/line_sum/pallas_call | solution.py:275
  111.6 1.4 %collective-permute-start.9 = (bf16[160,512]{1,0:T(8,128)(2,1)}, bf16[160,512]{1,0:T(8,128)(2,1)S(1)}, u32[]{:S(2)}, u32[]{:S(2)}) collective-permute-start(bf16[160,512]{1,0:T(8,128)(2,1)} %line_sum.1.refs_0_), channel_id=1, source_target_pairs={{0,24},{1,25},{2,26},{3,27},{4,28},{5,29},{6,30},{7,31},{8,16},{9,... | collective-permute-start | bytes 491528 | tf_op jit(solution)/shard_map/ppermute | solution.py:405
  113.0 1.4 collective-permute-start.8
  114.5 0.6 collective-permute-start.7
  115.1 4.6 %collective-permute-done.9.refs_3_ = bf16[160,512]{1,0:T(8,128)(2,1)S(1)} collective-permute-done((bf16[160,512]{1,0:T(8,128)(2,1)}, bf16[160,512]{1,0:T(8,128)(2,1)S(1)}, u32[]{:S(2)}, u32[]{:S(2)}) %collective-permute-start.9) | collective-permute-done | bytes 163872 | tf_op jit(solution)/shard_map/ppermute | solution.py:405
  119.6 1.7 %collective-permute-done.8.refs_2_ = bf16[160,512]{1,0:T(8,128)(2,1)S(1)} collective-permute-done((bf16[160,512]{1,0:T(8,128)(2,1)}, bf16[160,512]{1,0:T(8,128)(2,1)S(1)}, u32[]{:S(2)}, u32[]{:S(2)}) %collective-permute-start.8) | collective-permute-done | bytes 163872 | tf_op jit(solution)/shard_map/ppermute | solution.py:405
  121.4 0.5 collective-permute-start.11
  121.9 0.8 copy.48.refs_19_
  122.7 0.8 copy.49.refs_23_
  123.7 0.6 copy-done.5
  124.2 0.1 copy-done.6
  124.4 0.1 copy-done.8
  124.4 15.4 %update.1 = (f32[602,512]{1,0:T(8,128)}, f32[1,2,512,512]{3,2,1,0:T(8,128)}, f32[1,1024,512]{2,1,0:T(8,128)}, f32[512,41]{1,0:T(8,128)}, f32[602,512]{1,0:T(8,12...) custom-call(s32[2]{0:T(128)} %pad_add_fusion.me, ...), custom_call_target="tpu_custom_call" | custom-call | tf_op jit(solution)/shard_map/update/pallas_call | solution.py:371
  139.8 1.7 %copy.50 = f32[512,41]{0,1:T(8,128)} copy(f32[512,41]{1,0:T(8,128)} %get-tuple-element.87) | data formatting | bytes 167936
  141.5 1.7 %copy.51 = f32[512,41]{0,1:T(8,128)} copy(f32[512,41]{1,0:T(8,128)} %get-tuple-element.91) | data formatting | bytes 167936
  143.3 1.7 %copy.52 = f32[512,41]{0,1:T(8,128)} copy(f32[512,41]{1,0:T(8,128)} %get-tuple-element.95) | data formatting | bytes 167936
  (41 shorter events, 0.1 us)
Async XLA Ops:
  6.5 23.5 %all-to-all-start = ((bf16[32,8,640]{2,1,0:T(8,128)(2,1)}), bf16[32,8,640]{2,1,0:T(8,128)(2,1)S(1)}, u32[]{:S(2)}, u32[]{:S(2)}) async-start(bf16[32,8,640]{2,1,0:T(8,128)(2,1)} %pad_bitcast_fusion), calls=%async_computation | async-start | bytes 655360 | tf_op jit(solution)/shard_map/all_to_all | solution.py:412
  13.8 7.8 %copy-start.18 = (s32[32,12]{0,1:T(8,128)S(1)}, s32[32,12]{0,1:T(8,128)}, u32[]{:S(2)}) copy-start(s32[32,12]{0,1:T(8,128)} %param.19) | copy-start | bytes 4612
  13.9 8.6 %copy-start.15 = (f32[512,41]{0,1:T(8,128)S(1)}, f32[512,41]{0,1:T(8,128)}, u32[]{:S(2)}) copy-start(f32[512,41]{0,1:T(8,128)} %param.27) | copy-start | bytes 251908
  30.0 0.7 copy-start
  71.8 50.1 %copy-start.16 = (f32[512,41]{0,1:T(8,128)S(1)}, f32[512,41]{0,1:T(8,128)}, u32[]{:S(2)}) copy-start(f32[512,41]{0,1:T(8,128)} %param.31) | copy-start | bytes 251908
  71.8 51.0 %copy-start.17 = (f32[512,41]{0,1:T(8,128)S(1)}, f32[512,41]{0,1:T(8,128)}, u32[]{:S(2)}) copy-start(f32[512,41]{0,1:T(8,128)} %param.35) | copy-start | bytes 251908
  71.8 2.4 %collective-permute-start = (bf16[4,160,512]{2,1,0:T(8,128)(2,1)}, bf16[4,160,512]{2,1,0:T(8,128)(2,1)S(1)}, u32[]{:S(2)}, u32[]{:S(2)}) collective-permute-start(bf16[4,160,512]{2,1,0:T(8,128)(2,1)} %get-tuple-element.45), channel_id=1, source_target_pairs={{0,4},{1,5},{2,6},{3,7},{4,0},{5,1},{6,2},{7,3},{8,12},{9,13},{10,... | collective-permute-start | bytes 1966088 | tf_op jit(solution)/shard_map/ppermute | solution.py:405
  74.1 0.8 copy-start.1
  77.4 7.2 %collective-permute-start.1 = (bf16[160,512]{1,0:T(8,128)(2,1)}, bf16[160,512]{1,0:T(8,128)(2,1)S(1)}, u32[]{:S(2)}, u32[]{:S(2)}) collective-permute-start(bf16[160,512]{1,0:T(8,128)(2,1)} %get-tuple-element.47), channel_id=1, source_target_pairs={{0,8},{1,9},{2,10},{3,11},{4,12},{5,13},{6,14},{7,15},{8,0},{9,1},... | collective-permute-start | bytes 491528 | tf_op jit(solution)/shard_map/ppermute | solution.py:405
  79.2 9.7 %collective-permute-start.2 = (bf16[160,512]{1,0:T(8,128)(2,1)}, bf16[160,512]{1,0:T(8,128)(2,1)S(1)}, u32[]{:S(2)}, u32[]{:S(2)}) collective-permute-start(bf16[160,512]{1,0:T(8,128)(2,1)} %get-tuple-element.48), channel_id=1, source_target_pairs={{0,16},{1,17},{2,18},{3,19},{4,20},{5,21},{6,22},{7,23},{8,24},{9,... | collective-permute-start | bytes 491528 | tf_op jit(solution)/shard_map/ppermute | solution.py:405
  80.7 8.2 %collective-permute-start.3 = (bf16[160,512]{1,0:T(8,128)(2,1)}, bf16[160,512]{1,0:T(8,128)(2,1)S(1)}, u32[]{:S(2)}, u32[]{:S(2)}) collective-permute-start(bf16[160,512]{1,0:T(8,128)(2,1)} %get-tuple-element.49), channel_id=1, source_target_pairs={{0,24},{1,25},{2,26},{3,27},{4,28},{5,29},{6,30},{7,31},{8,16},{9,... | collective-permute-start | bytes 491528 | tf_op jit(solution)/shard_map/ppermute | solution.py:405
  84.7 4.2 %copy-start.9 = (bf16[160,512]{1,0:T(8,128)(2,1)}, bf16[160,512]{1,0:T(8,128)(2,1)S(1)}, u32[]{:S(2)}) copy-start(bf16[160,512]{1,0:T(8,128)(2,1)S(1)} %collective-permute-done.1.refs_0_) | copy-start | bytes 491524
  88.9 0.7 copy-start.10
  88.9 0.7 copy-start.11
  91.5 9.1 %collective-permute-start.6 = (bf16[160,512]{1,0:T(8,128)(2,1)}, bf16[160,512]{1,0:T(8,128)(2,1)S(1)}, u32[]{:S(2)}, u32[]{:S(2)}) collective-permute-start(bf16[160,512]{1,0:T(8,128)(2,1)} %plane_sum.1.refs_0_), channel_id=1, source_target_pairs={{0,3},{1,2},{2,1},{3,0},{4,7},{5,6},{6,5},{7,4},{8,11},{9,10},{10,... | collective-permute-start | bytes 491528 | tf_op jit(solution)/shard_map/ppermute | solution.py:405
  94.9 13.4 %collective-permute-start.5 = (bf16[160,512]{1,0:T(8,128)(2,1)}, bf16[160,512]{1,0:T(8,128)(2,1)S(1)}, u32[]{:S(2)}, u32[]{:S(2)}) collective-permute-start(bf16[160,512]{1,0:T(8,128)(2,1)} %plane_sum.1.refs_0_), channel_id=1, source_target_pairs={{0,2},{1,3},{2,0},{3,1},{4,6},{5,7},{6,4},{7,5},{8,10},{9,11},{10,... | collective-permute-start | bytes 491528 | tf_op jit(solution)/shard_map/ppermute | solution.py:405
  94.9 13.4 %collective-permute-start.4 = (bf16[160,512]{1,0:T(8,128)(2,1)}, bf16[160,512]{1,0:T(8,128)(2,1)S(1)}, u32[]{:S(2)}, u32[]{:S(2)}) collective-permute-start(bf16[160,512]{1,0:T(8,128)(2,1)} %plane_sum.1.refs_0_), channel_id=1, source_target_pairs={{0,1},{1,0},{2,3},{3,2},{4,5},{5,4},{6,7},{7,6},{8,9},{9,8},{10,11... | collective-permute-start | bytes 491528 | tf_op jit(solution)/shard_map/ppermute | solution.py:405
  100.7 7.6 %copy-start.12 = (bf16[160,512]{1,0:T(8,128)(2,1)}, bf16[160,512]{1,0:T(8,128)(2,1)S(1)}, u32[]{:S(2)}) copy-start(bf16[160,512]{1,0:T(8,128)(2,1)S(1)} %collective-permute-done.6.refs_3_) | copy-start | bytes 491524
  108.3 0.7 copy-start.13
  109.0 0.7 copy-start.14
  111.6 8.1 %collective-permute-start.9 = (bf16[160,512]{1,0:T(8,128)(2,1)}, bf16[160,512]{1,0:T(8,128)(2,1)S(1)}, u32[]{:S(2)}, u32[]{:S(2)}) collective-permute-start(bf16[160,512]{1,0:T(8,128)(2,1)} %line_sum.1.refs_0_), channel_id=1, source_target_pairs={{0,24},{1,25},{2,26},{3,27},{4,28},{5,29},{6,30},{7,31},{8,16},{9,... | collective-permute-start | bytes 491528 | tf_op jit(solution)/shard_map/ppermute | solution.py:405
  113.0 8.3 %collective-permute-start.8 = (bf16[160,512]{1,0:T(8,128)(2,1)}, bf16[160,512]{1,0:T(8,128)(2,1)S(1)}, u32[]{:S(2)}, u32[]{:S(2)}) collective-permute-start(bf16[160,512]{1,0:T(8,128)(2,1)} %line_sum.1.refs_0_), channel_id=1, source_target_pairs={{0,16},{1,17},{2,18},{3,19},{4,20},{5,21},{6,22},{7,23},{8,24},{9,... | collective-permute-start | bytes 491528 | tf_op jit(solution)/shard_map/ppermute | solution.py:405
  114.5 6.9 %collective-permute-start.7 = (bf16[160,512]{1,0:T(8,128)(2,1)}, bf16[160,512]{1,0:T(8,128)(2,1)S(1)}, u32[]{:S(2)}, u32[]{:S(2)}) collective-permute-start(bf16[160,512]{1,0:T(8,128)(2,1)} %line_sum.1.refs_0_), channel_id=1, source_target_pairs={{0,8},{1,9},{2,10},{3,11},{4,12},{5,13},{6,14},{7,15},{8,0},{9,1},... | collective-permute-start | bytes 491528 | tf_op jit(solution)/shard_map/ppermute | solution.py:405
  115.1 8.5 %collective-permute-start.10 = (bf16[160,512]{1,0:T(8,128)(2,1)}, bf16[160,512]{1,0:T(8,128)(2,1)S(1)}, u32[]{:S(2)}, u32[]{:S(2)}) collective-permute-start(bf16[160,512]{1,0:T(8,128)(2,1)} %line_sum.1.refs_0_), channel_id=1, source_target_pairs={{0,4},{1,5},{2,6},{3,7},{4,0},{5,1},{6,2},{7,3},{8,12},{9,13},{10,... | collective-permute-start | bytes 491528 | tf_op jit(solution)/shard_map/ppermute | solution.py:405
  119.6 4.0 %copy-start.2 = (bf16[160,512]{1,0:T(8,128)(2,1)}, bf16[160,512]{1,0:T(8,128)(2,1)S(1)}, u32[]{:S(2)}) copy-start(bf16[160,512]{1,0:T(8,128)(2,1)S(1)} %collective-permute-done.9.refs_3_) | copy-start | bytes 491524
  119.6 3.9 %collective-permute-start.13 = (bf16[160,512]{1,0:T(8,128)(2,1)S(1)}, bf16[160,512]{1,0:T(8,128)(2,1)S(1)}, u32[]{:S(2)}, u32[]{:S(2)}) collective-permute-start(bf16[160,512]{1,0:T(8,128)(2,1)S(1)} %collective-permute-done.9.refs_3_), channel_id=1, source_target_pairs={{0,4},{1,5},{2,6},{3,7},{4,0},{5,1},{6,2},{7,3},{8,12},{9,13},{10,... | collective-permute-start | bytes 491528 | tf_op jit(solution)/shard_map/ppermute | solution.py:405
  121.4 2.3 %copy-start.3 = (bf16[160,512]{1,0:T(8,128)(2,1)}, bf16[160,512]{1,0:T(8,128)(2,1)S(1)}, u32[]{:S(2)}) copy-start(bf16[160,512]{1,0:T(8,128)(2,1)S(1)} %collective-permute-done.8.refs_2_) | copy-start | bytes 491524
  121.4 2.2 %collective-permute-start.12 = (bf16[160,512]{1,0:T(8,128)(2,1)S(1)}, bf16[160,512]{1,0:T(8,128)(2,1)S(1)}, u32[]{:S(2)}, u32[]{:S(2)}) collective-permute-start(bf16[160,512]{1,0:T(8,128)(2,1)S(1)} %collective-permute-done.8.refs_2_), channel_id=1, source_target_pairs={{0,4},{1,5},{2,6},{3,7},{4,0},{5,1},{6,2},{7,3},{8,12},{9,13},{10,... | collective-permute-start | bytes 491528 | tf_op jit(solution)/shard_map/ppermute | solution.py:405
  121.4 2.3 %copy-start.4 = (bf16[160,512]{1,0:T(8,128)(2,1)}, bf16[160,512]{1,0:T(8,128)(2,1)S(1)}, u32[]{:S(2)}) copy-start(bf16[160,512]{1,0:T(8,128)(2,1)S(1)} %collective-permute-done.7.refs_1_) | copy-start | bytes 491524
  121.4 2.2 %collective-permute-start.11 = (bf16[160,512]{1,0:T(8,128)(2,1)S(1)}, bf16[160,512]{1,0:T(8,128)(2,1)S(1)}, u32[]{:S(2)}, u32[]{:S(2)}) collective-permute-start(bf16[160,512]{1,0:T(8,128)(2,1)S(1)} %collective-permute-done.7.refs_1_), channel_id=1, source_target_pairs={{0,4},{1,5},{2,6},{3,7},{4,0},{5,1},{6,2},{7,3},{8,12},{9,13},{10,... | collective-permute-start | bytes 491528 | tf_op jit(solution)/shard_map/ppermute | solution.py:405
  123.6 0.7 copy-start.5
  123.6 0.7 copy-start.6
  123.6 0.8 copy-start.7
  123.6 0.8 copy-start.8
